TPU v7x, 32 devices: a whole 2x2x4 slice. The times are simulated.
32 devices in a mesh: pole: 2 (over y), row: 4 (over z), col: 4 (over x, core).
Axes of the slice: x: 2, y: 2, z: 4, core: 2. Of those that a mesh axis runs over, the one named last changes fastest.
Arguments:
- ancestors: bfloat16 [4096, 2048], P(('pole', 'row'), 'col'), parts along dimension 0, may hold values from -6 to 6
- panel: bfloat16 [4, 4096, 256], P(None, ('pole', 'row')), parts along dimension 1, may hold values from -0.125 to 0.125
- coupling: bfloat16 [6, 256, 256], P('pole'), parts along dimension 0, may hold values from -0.375 to 0.375
- pivots: bfloat16 [8, 256, 256], P('pole'), parts along dimension 0, may hold values from -6 to 6
- tile_lists: int32 [4, 8], replicated, may hold values from 0 to 8, as said below
Outputs:
- columns: float32 [4, 4096, 256], P(None, ('pole', 'row', 'col')), parts along dimension 1
- diagonal_blocks: float32 [8, 256, 256], P('pole', 'col'), parts along dimension 0
- linking_blocks: float32 [6, 256, 256], P('pole', 'col'), parts along dimension 0
There are 2 independent parts, one for each index of `pole`. A program takes and returns all parts, laid end to end along the dimension named above; an argument that names none is the same for every part. Nothing has to cross between parts.
Inputs may be any that keep to these rules, and one draw needn't show every extreme that they name: `tile_lists`: each row lists distinct tiles of the region first, then is padded with 8; the tiles of row s + 1 are among those of row s, and row 0 names every tile; each row names at least half of the tiles.
All inputs are finite; a program needn't handle non-finite values.
Results may differ from a plain program's by a relative error of at most 0.0003.
Values may be sent and summed in bfloat16 or wider, within the bound.
A program may use at most 64 MiB of HBM per device.

v0:
```python
import jax
import jax.numpy as jnp
from jax import lax
from jax.sharding import PartitionSpec as P


def broadcast(block, axis, owner):
    block = jnp.where(lax.axis_index(axis) == owner, block, jnp.zeros_like(block))
    return lax.psum(block, axis)


def membership(tile_lists, tile_ids):
    return jnp.any(tile_lists[:, :, None] == tile_ids[None, None, :], axis=1)


def shards(ancestors, panel, coupling, pivots, tile_lists):
    supernodes, rows_local, block_width = panel.shape
    row_count = lax.axis_size("row")
    col_count = lax.axis_size("col")
    row_index = lax.axis_index("row")
    col_index = lax.axis_index("col")
    highest = lax.Precision.HIGHEST
    local_tiles = (row_index * rows_local + jnp.arange(rows_local, dtype=jnp.int32)) // block_width
    in_list = membership(tile_lists, local_tiles)
    masked = jnp.where(in_list[:, :, None], panel, jnp.zeros((), panel.dtype))
    root_count = row_count // col_count

    def accumulate(root_step, running):
        arrived = broadcast(masked, "row", col_index * root_count + root_step)
        anc_block = lax.dynamic_slice_in_dim(ancestors, root_step * rows_local, rows_local, 1)
        return running + jnp.einsum(
            "ik,skj->sij", anc_block, arrived, preferred_element_type=jnp.float32
        )

    partial_value = lax.fori_loop(
        0, root_count, accumulate, jnp.zeros((supernodes, rows_local, block_width), jnp.float32)
    )
    share_out = rows_local // col_count
    reduced = lax.psum(partial_value, "col")
    column_list = []
    gram_parts = []
    cross_parts = []
    previous = None
    for sup_idx in range(supernodes):
        image_rows = reduced[sup_idx]
        if sup_idx > 0:
            image_rows = image_rows + jnp.dot(
                previous, coupling[sup_idx - 1].astype(jnp.float32), precision=highest
            )
        column_out = jnp.where(in_list[sup_idx][:, None], -image_rows, jnp.float32(0.0))
        piece_f = masked[sup_idx].astype(jnp.float32)
        gram_parts.append(jnp.einsum("ki,kj->ij", piece_f, column_out, precision=highest))
        if sup_idx > 0:
            cross_parts.append(jnp.einsum("ki,kj->ij", previous, piece_f, precision=highest))
        column_list.append(column_out)
        previous = column_out
    gram_local = jnp.stack(gram_parts)
    cross_local = jnp.stack(cross_parts)
    gram_all, cross_all = lax.psum((gram_local, cross_local), "row")
    diagonals = []
    linking = []
    for sup_idx in range(supernodes):
        pivot_f = pivots[sup_idx].astype(jnp.float32)
        if sup_idx > 0:
            link_f = coupling[sup_idx - 1].astype(jnp.float32)
            linked = -(cross_all[sup_idx - 1] + jnp.dot(diagonals[-1], link_f, precision=highest))
            linking.append(linked)
            diagonals.append(
                pivot_f
                - gram_all[sup_idx]
                - jnp.einsum("ki,kj->ij", link_f, linked, precision=highest)
            )
        else:
            diagonals.append(pivot_f - gram_all[sup_idx])
    columns = jnp.stack(column_list)
    columns = lax.dynamic_slice_in_dim(columns, col_index * share_out, share_out, 1)
    block_share = block_width // col_count
    diagonal_blocks = lax.dynamic_slice_in_dim(
        jnp.stack(diagonals), col_index * block_share, block_share, 1
    )
    linking_blocks = lax.dynamic_slice_in_dim(
        jnp.stack(linking), col_index * block_share, block_share, 1
    )
    return (columns, diagonal_blocks, linking_blocks)


def solution(mesh):
    placed = (
        P(("pole", "row"), "col"),
        P(None, ("pole", "row"), None),
        P("pole", None, None),
        P("pole", None, None),
        P(),
    )
    return jax.shard_map(
        shards,
        mesh=mesh,
        in_specs=placed,
        out_specs=(
            P(None, ("pole", "row", "col"), None),
            P("pole", "col", None),
            P("pole", "col", None),
        ),
        check_vma=False,
    )
```

profile of v0, /device:TPU:0, one launch (start us, length us, event | category | flops | bytes accessed | tf_op | source)
XLA Modules:
  0.0 218.5 jit_solution(14658062876767883981)
XLA Ops:
  7.2 0.0 copy-start
  7.2 0.0 copy-start.8
  7.2 0.0 all-reduce.5.cloned.1.call-start
  7.2 1.5 copy.13
  8.8 0.0 copy-done.8
  8.8 0.1 compare_reduce_fusion
  8.9 1.1 broadcast_select_fusion.1
  10.1 0.0 all-reduce.5.cloned.1.call-update
  10.1 0.0 all-reduce.7.cloned.1.call-start
  10.1 54.8 %all-reduce.5.cloned.1.call-done = bf16[4,512,256]{1,2,0:T(8,128)(2,1)} async-done(((bf16[4,512,256]{1,2,0:T(8,128)(2,1)}), bf16[4,512,256]{1,2,0:T(8,128)(2,1)}) %all-reduce.5.cloned.1.call-update) | async-done | bytes 1048592 | tf_op jit(solution)/shard_map/while/body/eval_jaxpr/psum | solution.py:9
  64.9 0.0 copy-done
  64.9 3.3 %convolution_bitcast_fusion = f32[4,512,256]{1,2,0:T(8,128)} fusion(bf16[4,512,256]{1,2,0:T(8,128)(2,1)} %all-reduce.5.cloned.1.call-done, bf16[512,512]{1,0:T(8,128)(2,1)S(1)} %copy-done), kind=kOutput, calls=%fused_computation.4 | convolution fusion | flops 536870912 | bytes 3670016 | tf_op jit(solution)/shard_map/while/body/eval_jaxpr/ik,skj->sij/dot_general | solution.py:31
  68.3 0.0 all-reduce.7.cloned.1.call-update
  68.3 0.0 all-reduce.9.cloned.1.call-start
  68.4 50.8 %all-reduce.7.cloned.1.call-done = f32[4,512,256]{1,2,0:T(8,128)} async-done(((f32[4,512,256]{1,2,0:T(8,128)}), f32[4,512,256]{1,2,0:T(8,128)}) %all-reduce.7.cloned.1.call-update) | async-done | bytes 2097168 | tf_op jit(solution)/shard_map/psum | solution.py:39
  119.2 1.2 fusion.16
  120.5 0.4 convolution_bitcast_fusion.10
  120.9 0.0 copy-done.3
  120.9 0.0 copy-done.4
  121.0 0.5 fusion.5
  121.4 0.4 convolution_bitcast_fusion.9
  121.9 0.5 fusion.3
  122.4 0.4 convolution_bitcast_fusion.8
  122.8 0.4 convolution_bitcast_fusion.4
  123.2 0.4 convolution_bitcast_fusion.5
  123.7 0.4 convolution_bitcast_fusion.6
  124.1 0.5 fusion.1
  124.6 0.0 copy-start.1
  124.6 0.4 convolution_bitcast_fusion.7
  125.0 0.3 copy-done.1
  125.3 0.9 pad_maximum_fusion.1
  126.3 1.1 pad_maximum_fusion
  127.4 0.0 all-reduce.9.cloned.1.call-update
  127.4 0.1 copy-done.2
  127.5 0.1 fusion.15
  127.6 0.0 copy-start.7
  127.6 1.0 copy.17
  128.6 77.1 %all-reduce.9.cloned.1.call-done = (f32[4,256,256]{2,1,0:T(8,128)}, f32[3,256,256]{2,1,0:T(8,128)}) async-done(((f32[4,256,256]{2,1,0:T(8,128)}, f32[3,256,256]{2,1,0:T(8,128)}), (f32[4,256,256]{2,1,0:T(8,128)}, f32[3,256,256]{2,1,0:T(8,128)})) %all-reduce.9.cloned.1.call-update) | async-done | bytes 1835024 | tf_op jit(solution)/shard_map/psum | solution.py:59
  205.7 1.1 slice_subtract_fusion.3
  206.8 1.2 fusion.12
  208.0 1.3 fusion.11
  209.3 0.3 fusion.10
  209.6 0.0 copy-done.5
  209.6 0.3 fusion.9
  209.9 0.3 fusion.8
  210.2 0.3 fusion.7
  210.6 0.7 fusion.23
  211.3 0.7 fusion.29
  (9 shorter events, 0.1 us)
Async XLA Ops:
  7.2 57.8 %copy-start = (bf16[512,512]{1,0:T(8,128)(2,1)S(1)}, bf16[512,512]{1,0:T(8,128)(2,1)}, u32[]{:S(2)}) copy-start(bf16[512,512]{1,0:T(8,128)(2,1)} %param.5) | copy-start | bytes 1572868
  7.2 1.6 copy-start.8
  7.2 57.8 %all-reduce.5.cloned.1.call-start = ((), (), s32[]{:S(2)}) async-start(), calls=%async_computation | async-start | bytes 2097152 | tf_op jit(solution)/shard_map/while/body/eval_jaxpr/psum | solution.py:9
  10.1 109.1 %all-reduce.7.cloned.1.call-start = ((), (), s32[]{:S(2)}) async-start(), calls=%async_computation.1 | async-start | bytes 4194304 | tf_op jit(solution)/shard_map/psum | solution.py:39
  68.3 52.7 %copy-start.3 = (bf16[3,256,256]{2,1,0:T(8,128)(2,1)S(1)}, bf16[3,256,256]{2,1,0:T(8,128)(2,1)}, u32[]{:S(2)}) copy-start(bf16[3,256,256]{2,1,0:T(8,128)(2,1)} %param.7) | copy-start | bytes 1179652
  68.3 137.4 %all-reduce.9.cloned.1.call-start = ((), (), s32[]{:S(2)}) async-start(), calls=%async_computation.2 | async-start | bytes 3670016 | tf_op jit(solution)/shard_map/psum | solution.py:59
  119.2 1.7 copy-start.4
  124.6 0.8 copy-start.1
  126.3 1.2 copy-start.2
  127.6 80.5 %copy-start.7 = (bf16[4,256,256]{2,1,0:T(8,128)(2,1)S(1)}, bf16[4,256,256]{2,1,0:T(8,128)(2,1)}, u32[]{:S(2)}) copy-start(bf16[4,256,256]{2,1,0:T(8,128)(2,1)} %param.8) | copy-start | bytes 1572868
  205.7 3.7 %copy-start.6 = (f32[3,256,256]{2,1,0:T(8,128)S(1)}, f32[3,256,256]{2,1,0:T(8,128)}, u32[]{:S(2)}) copy-start(f32[3,256,256]{2,1,0:T(8,128)} %get-tuple-element.32) | copy-start | bytes 2359300
  205.7 3.9 %copy-start.5 = (f32[4,256,256]{2,1,0:T(8,128)S(1)}, f32[4,256,256]{2,1,0:T(8,128)}, u32[]{:S(2)}) copy-start(f32[4,256,256]{2,1,0:T(8,128)} %get-tuple-element.31) | copy-start | bytes 3145732
Sparse Core Ops, SparseCore 0:
  10.4 54.5 all-reduce.4
  68.4 50.7 all-reduce.6
  127.5 78.0 all-reduce.8
where the time goes:
time: 219 us
  waiting for transfers between devices  183 us (84%)
  between operations  14 us (6%)
  matrix products  11.4 us (5%)
  other arithmetic  7.15 us (3%)
  local copies, waits for them, and re-layouts  3.05 us (1%)
    psum x1, waiting for transfers between devices, shards(): gram_all, cross_all = lax.psum((gram_local, cross_local), 'row')  77.1 us
    psum x1, waiting for transfers between devices, broadcast(): return lax.psum(block, axis)  54.8 us
    psum x1, waiting for transfers between devices, shards(): reduced = lax.psum(partial_value, 'col')  50.8 us
  transfers between devices with their start and end apart: 3, of which 3 were waited for; matrix products, arithmetic and copies ran while one was open for 1% of the time, Pallas kernels for 0%

commit v1 on v0

v1 whole, which is shorter than its diff:
```python
import functools

import jax
import jax.numpy as jnp
from jax import lax
from jax.experimental import pallas as pl
from jax.experimental.pallas import tpu as pltpu
from jax.sharding import PartitionSpec as P

F32 = jnp.float32
BF16 = jnp.bfloat16
MESH = pl.DeviceIdType.MESH
CORES = 2


def dot(a, b):
    return lax.dot_general(a, b, (((1,), (0,)), ((), ())), preferred_element_type=F32)


def dot_t(a, b):
    return lax.dot_general(a, b, (((0,), (0,)), ((), ())), preferred_element_type=F32)


def split(x):
    hi = x.astype(BF16)
    return hi, (x - hi.astype(F32)).astype(BF16)


def kernel(
    rows, cols,
    anc_hbm, panel_hbm, coup_hbm, piv_hbm, lists,
    out_col, out_dia, out_link,
    anc, masked, coup, piv, load_sem,
    held, via, colbuf, blkbuf, col_a, blk_a, col_b, blk_b, z_in, z_mid,
    hi_buf, lo_buf,
    own_up, own_dn, own_rx, via_up, via_dn, via_rx, cross_tx, cross_rx,
    cola_tx, cola_rx, blka_tx, blka_rx, colb_tx, colb_rx, blkb_tx, blkb_rx,
    zi_tx, zo_tx, zin_rx, zmid_rx,
):
    sups, rows_local, width = masked.shape
    half = rows_local // 2
    q = rows // cols
    nx = cols // CORES
    share = rows_local // cols
    band = width // cols
    pieces = 2 * sups - 1
    r = lax.axis_index("row")
    c = lax.axis_index("col")
    x = c // CORES
    k = c % CORES
    mate = x * CORES + (1 - k)
    other = (x + 1 - 2 * (x % 2)) * CORES + k
    mid = rows // 2
    low = r < mid
    inner = jnp.where(low, r + 1, r - 1)
    outer = jnp.where(low, r - 1, r + 1)
    is_mid = jnp.logical_or(r == mid - 1, r == mid)
    has_outer = jnp.logical_and(r > 0, r < rows - 1)

    loads = [
        pltpu.make_async_copy(src, dst, load_sem.at[i])
        for i, (src, dst) in enumerate(
            [(panel_hbm, masked), (anc_hbm, anc), (coup_hbm, coup), (piv_hbm, piv)]
        )
    ]
    for load in loads:
        load.start()

    barrier = pltpu.get_barrier_semaphore()

    def greet(row, col):
        pl.semaphore_signal(barrier, inc=1, device_id={"row": row, "col": col}, device_id_type=MESH)

    @pl.when(r > 0)
    def _():
        greet(r - 1, c)

    @pl.when(r < rows - 1)
    def _():
        greet(r + 1, c)

    greet(r, mate)
    for dx in range(1, nx):
        greet(r, lax.rem(x + dx, nx) * CORES + k)

    tiles = rows_local // width
    names = lists[...]
    member = []
    for t in range(tiles):
        tile = r * tiles + t
        member.append(jnp.max(jnp.where(names == tile, F32(1), F32(0)), axis=1, keepdims=True))
    loads[0].wait()
    for s in range(sups):
        for t in range(tiles):
            sl = pl.ds(t * width, width)
            m = member[t][s:s + 1, :].astype(BF16)
            masked[s, sl, :] = masked[s, sl, :] * m

    for j in range(q):
        @pl.when(c * q + j == r)
        def _():
            for s in range(sups):
                held[j, s, 0] = masked[s, 0:half, :]
                held[j, s, 1] = masked[s, half:, :]

        @pl.when(other * q + j == r)
        def _():
            for s in range(sups):
                via[j, s] = masked[s, half:, :]

    pl.semaphore_wait(
        barrier,
        jnp.where(r > 0, 1, 0) + jnp.where(r < rows - 1, 1, 0) + nx,
    )

    def remote(src, dst, tx, rx, row, col):
        return pltpu.make_async_remote_copy(
            src_ref=src, dst_ref=dst, send_sem=tx, recv_sem=rx,
            device_id={"row": row, "col": col}, device_id_type=MESH,
        )

    def own_copy(j, s, tx, row):
        ref = held.at[j, s, 0]
        return remote(ref, ref, tx.at[j, s], own_rx.at[j, s], row, c)

    def via_copy(j, s, tx, row):
        ref = via.at[j, s]
        return remote(ref, ref, tx.at[j, s], via_rx.at[j, s], row, c)

    def cross_copy(j, s):
        return remote(via.at[j, s], held.at[j, s, 1], cross_tx.at[j, s], cross_rx.at[j, s], r, other)

    def service(s):
        for j in range(q):
            for maker, first, up, dn, crossing in (
                (via_copy, other * q + j, via_up, via_dn, True),
                (own_copy, c * q + j, own_up, own_dn, False),
            ):
                @pl.when(first != r)
                def _():
                    maker(j, s, up, r).wait_recv()

                @pl.when(jnp.logical_and(first <= r, r < rows - 1))
                def _():
                    maker(j, s, up, r + 1).start()

                @pl.when(jnp.logical_and(first >= r, r > 0))
                def _():
                    maker(j, s, dn, r - 1).start()

                if crossing:
                    @pl.when(first != r)
                    def _():
                        cross_copy(j, s).start()

    def col_a_copy(s):
        return remote(colbuf.at[s, 1 - k], col_a.at[s], cola_tx.at[s], cola_rx.at[s], r, mate)

    def blk_a_copy(i):
        return remote(blkbuf.at[i, 1 - k], blk_a.at[i], blka_tx.at[i], blka_rx.at[i], r, mate)

    def col_b_copy(s, dx):
        to = lax.rem(x + dx, nx)
        return remote(colbuf.at[s, k, to], col_b.at[s, dx - 1], colb_tx.at[s, dx - 1],
                      colb_rx.at[s, dx - 1], r, to * CORES + k)

    def blk_b_copy(i, dx):
        to = lax.rem(x + dx, nx)
        return remote(blkbuf.at[i, k, to], blk_b.at[i, dx - 1], blkb_tx.at[i, dx - 1],
                      blkb_rx.at[i, dx - 1], r, to * CORES + k)

    here = jnp.where(jnp.logical_and(r == 0, c == 0), F32(1), F32(0))

    def put_piece(i, value):
        for to in range(cols):
            blkbuf[i, to % CORES, to // CORES] = value[to * band:(to + 1) * band, :]
        blk_a_copy(i).start()

    def compute(s, before):
        for j in range(q):
            @pl.when(c * q + j != r)
            def _():
                cross_copy(j, s).wait_recv()
        if s == 0:
            loads[1].wait()
            loads[2].wait()
            loads[3].wait()
        image = None
        for j in range(q):
            block = held[j, s].reshape(rows_local, width)
            term = dot(anc[:, j * rows_local:(j + 1) * rows_local], block)
            image = term if image is None else image + term
        if s > 0:
            link = coup[s - 1]
            image = image + dot(hi_buf[s - 1], link) + dot(lo_buf[s - 1], link)
        for t in range(tiles):
            sl = slice(t * width, (t + 1) * width)
            value = image[sl, :] * (-member[t][s:s + 1, :])
            hi, lo = split(value)
            hi_buf[s, sl, :] = hi
            lo_buf[s, sl, :] = lo
            per = width // share
            for u in range(per):
                to = t * per + u
                colbuf[s, to % CORES, to // CORES] = value[u * share:(u + 1) * share, :]
        col_a_copy(s).start()
        piece = masked[s]
        gram = dot_t(piece, hi_buf[s]) + dot_t(piece, lo_buf[s])
        base = piv[s].astype(F32) * here - gram
        if s == 0:
            diag = base
        else:
            cross = dot_t(hi_buf[s - 1], piece) + dot_t(lo_buf[s - 1], piece)
            hi, lo = split(before)
            linked = -(cross + dot(hi, link) + dot(lo, link))
            put_piece(2 * s - 1, linked)
            hi, lo = split(linked)
            diag = base - (dot_t(link, hi) + dot_t(link, lo))
        put_piece(2 * s, diag)
        return diag

    def blk_to_x(i):
        blk_a_copy(i).wait_recv()
        blkbuf[i, k] = blkbuf[i, k] + blk_a[i]
        for dx in range(1, nx):
            blk_b_copy(i, dx).start()

    def col_to_x(s):
        col_a_copy(s).wait_recv()
        colbuf[s, k] = colbuf[s, k] + col_a[s]
        for dx in range(1, nx):
            col_b_copy(s, dx).start()

    service(0)
    service(1)
    diag = compute(0, None)
    service(2)
    diag = compute(1, diag)
    blk_to_x(0)
    for s in range(3, sups):
        service(s)
    for s in range(2, sups):
        diag = compute(s, diag)
        blk_to_x(2 * s - 3)
        blk_to_x(2 * s - 2)
    blk_to_x(pieces - 2)
    blk_to_x(pieces - 1)
    for s in range(sups):
        col_to_x(s)

    def to_inner(i, dst, rx):
        return remote(blkbuf.at[i, k, x], dst.at[i], zi_tx.at[i], rx.at[i], inner, c)

    def result(i):
        return out_dia.at[i // 2] if i % 2 == 0 else out_link.at[i // 2]

    def to_outer(i):
        return remote(result(i), z_mid.at[i], zo_tx.at[i], zmid_rx.at[i], outer, c)

    def z_inward(i):
        total = blkbuf[i, k, x]
        for dx in range(1, nx):
            blk_b_copy(i, dx).wait_recv()
            total = total + blk_b[i, dx - 1]
        blkbuf[i, k, x] = total

        @pl.when(has_outer)
        def _():
            to_inner(i, z_in, zin_rx).wait_recv()
            blkbuf[i, k, x] = blkbuf[i, k, x] + z_in[i]

        @pl.when(is_mid)
        def _():
            to_inner(i, z_mid, zmid_rx).start()

        @pl.when(jnp.logical_not(is_mid))
        def _():
            to_inner(i, z_in, zin_rx).start()

    def z_outward(i):
        to_outer(i).wait_recv()

        @pl.when(is_mid)
        def _():
            result(i)[...] = blkbuf[i, k, x] + z_mid[i]

        @pl.when(jnp.logical_not(is_mid))
        def _():
            result(i)[...] = z_mid[i]

        @pl.when(has_outer)
        def _():
            to_outer(i).start()

    lag = 2
    for i in range(pieces + lag):
        if i < pieces:
            z_inward(i)
        if i >= lag:
            z_outward(i - lag)

    for s in range(sups):
        total = colbuf[s, k, x]
        for dx in range(1, nx):
            col_b_copy(s, dx).wait_recv()
            total = total + col_b[s, dx - 1]
        out_col[s] = total

    for s in range(sups):
        for j in range(q):
            for maker, first, up, dn, crossing in (
                (via_copy, other * q + j, via_up, via_dn, True),
                (own_copy, c * q + j, own_up, own_dn, False),
            ):
                @pl.when(jnp.logical_and(first <= r, r < rows - 1))
                def _():
                    maker(j, s, up, r + 1).wait_send()

                @pl.when(jnp.logical_and(first >= r, r > 0))
                def _():
                    maker(j, s, dn, r - 1).wait_send()

                if crossing:
                    @pl.when(first != r)
                    def _():
                        cross_copy(j, s).wait_send()
        col_a_copy(s).wait_send()
        for dx in range(1, nx):
            col_b_copy(s, dx).wait_send()
    for i in range(pieces):
        blk_a_copy(i).wait_send()
        for dx in range(1, nx):
            blk_b_copy(i, dx).wait_send()
        to_inner(i, z_in, zin_rx).wait_send()

        @pl.when(has_outer)
        def _():
            to_outer(i).wait_send()


def shards(rows, cols, ancestors, panel, coupling, pivots, tile_lists):
    sups, rows_local, width = panel.shape
    q = rows // cols
    nx = cols // CORES
    share = rows_local // cols
    band = width // cols
    pieces = 2 * sups - 1
    half = rows_local // 2
    dma = lambda *shape: pltpu.SemaphoreType.DMA(shape)
    hbm = pl.BlockSpec(memory_space=pl.ANY)
    vmem = pl.BlockSpec(memory_space=pltpu.VMEM)
    return pl.pallas_call(
        functools.partial(kernel, rows, cols),
        out_shape=(
            jax.ShapeDtypeStruct((sups, share, width), F32),
            jax.ShapeDtypeStruct((sups, band, width), F32),
            jax.ShapeDtypeStruct((sups - 1, band, width), F32),
        ),
        in_specs=[hbm, hbm, hbm, hbm, vmem],
        out_specs=(vmem, vmem, vmem),
        scratch_shapes=[
            pltpu.VMEM(ancestors.shape, BF16),
            pltpu.VMEM(panel.shape, BF16),
            pltpu.VMEM(coupling.shape, BF16),
            pltpu.VMEM(pivots.shape, BF16),
            dma(4),
            pltpu.VMEM((q, sups, 2, half, width), BF16),
            pltpu.VMEM((q, sups, half, width), BF16),
            pltpu.VMEM((sups, CORES, nx, share, width), F32),
            pltpu.VMEM((pieces, CORES, nx, band, width), F32),
            pltpu.VMEM((sups, nx, share, width), F32),
            pltpu.VMEM((pieces, nx, band, width), F32),
            pltpu.VMEM((sups, nx - 1, share, width), F32),
            pltpu.VMEM((pieces, nx - 1, band, width), F32),
            pltpu.VMEM((pieces, band, width), F32),
            pltpu.VMEM((pieces, band, width), F32),
            pltpu.VMEM((sups, rows_local, width), BF16),
            pltpu.VMEM((sups, rows_local, width), BF16),
            dma(q, sups), dma(q, sups), dma(q, sups),
            dma(q, sups), dma(q, sups), dma(q, sups),
            dma(q, sups), dma(q, sups),
            dma(sups), dma(sups), dma(pieces), dma(pieces),
            dma(sups, nx - 1), dma(sups, nx - 1), dma(pieces, nx - 1), dma(pieces, nx - 1),
            dma(pieces), dma(pieces), dma(pieces), dma(pieces),
        ],
        compiler_params=pltpu.CompilerParams(
            collective_id=0, has_side_effects=True, vmem_limit_bytes=56 * 1024 * 1024
        ),
    )(ancestors, panel, coupling, pivots, tile_lists)


def solution(mesh):
    placed = (
        P(("pole", "row"), "col"),
        P(None, ("pole", "row"), None),
        P("pole", None, None),
        P("pole", None, None),
        P(),
    )
    return jax.shard_map(
        functools.partial(shards, mesh.shape["row"], mesh.shape["col"]),
        mesh=mesh,
        in_specs=placed,
        out_specs=(
            P(None, ("pole", "row", "col"), None),
            P("pole", "col", None),
            P("pole", "col", None),
        ),
        check_vma=False,
    )
```

time: 219 us -> 128 us (0.58)
  waiting for transfers between devices: 183 us -> 0 us
  Pallas kernels: 0 us -> 123 us
  between operations: 14 us -> 0.65 us
  matrix products: 11.4 us -> 0 us
  other arithmetic: 7.15 us -> 0 us
    psum x3 -> x0, waiting for transfers between devices: 183 us -> none  [the longest x1 77.1 us: shards(): gram_all, cross_all = lax.psum((gram_local, cross_local), 'row')]
    pallas_call x0 -> x1, Pallas kernels: none -> 123 us  [shards(): pl.pallas_call(functools.partial(kernel, rows, cols), out_shape=(jax.Shap...]
    dot_general x17 -> x0, matrix products: 11.4 us -> none  [the longest x1 3.31 us: accumulate(): jnp.einsum('ik,skj->sij', anc_block, arrived, preferred_element_type=jnp....]
    another operation x5 -> x0, other arithmetic: 3.52 us -> none  [the longest x1 1.1 us: shards(): gram_local = jnp.stack(gram_parts)]
    select_n x3 -> x0, other arithmetic: 2.39 us -> none  [the longest x1 1.25 us: shards(): jnp.where(in_list[sup_idx][:, None], -image_rows, jnp.float32(0.0))]
  transfers between devices with their start and end apart: 3 -> 0, of which waited for: 3 -> 0; matrix products, arithmetic and copies ran while one was open for 1% -> 0% of each run, Pallas kernels for 0% -> 0%
where the time goes in v1:
time: 128 us; the launch traced here: 127 us
  Pallas kernels  123 us (96%)
  local copies, waits for them, and re-layouts  3.61 us (3%)
    pallas_call x1, Pallas kernels, shards(): pl.pallas_call(functools.partial(kernel, rows, cols), out_shape=(jax.Shap...  123 us
    unnamed x7, local copies, waits for them, and re-layouts  3.61 us

profile of v1, /device:TPU:0, one launch (start us, length us, event | category | flops | bytes accessed | tf_op | source)
XLA Modules:
  0.0 127.5 jit_solution(14276816716113335938)
XLA Ops:
  0.6 123.2 %shard_map.76 = (f32[4,128,256]{2,1,0:T(8,128)}, f32[4,64,256]{2,1,0:T(8,128)}, f32[3,64,256]{2,1,0:T(8,128)}) custom-call(bf16[512,512]{1,0:T(8,128)(2,1)} %anc_hbm.1, bf16[4,512,256]{2,1,0:T(8,128)(2,1)} %panel_hbm.1, bf16[3,256,256]{2,1,0:T(8,128)(2,1)} %coup_hbm.1, bf16[4,256,256]{2,1,0:T(8,128)(2,1)} %piv_hbm.1, s32[4,8]{1,0:T(4,128)} %lists.1), custom_call_target="tpu_custom_call" | custom-call | tf_op jit(solution)/shard_map/pallas_call | solution.py:352
  123.8 0.0 copy-start
  123.9 1.9 %copy.11 = f32[4,128,256]{2,1,0:T(8,128)} copy(f32[4,128,256]{2,1,0:T(8,128)} %get-tuple-element.6) | data formatting | bytes 1048576
  125.8 0.0 copy-done
  125.8 0.0 copy-start.1
  125.8 0.7 copy.12
  126.5 0.3 copy-done.1
  126.8 0.7 copy.13
Async XLA Ops:
  123.8 1.9 %copy-start = (f32[4,64,256]{2,1,0:T(8,128)S(1)}, f32[4,64,256]{2,1,0:T(8,128)}, u32[]{:S(2)}) copy-start(f32[4,64,256]{2,1,0:T(8,128)} %get-tuple-element.7) | copy-start | bytes 786436
  125.8 1.0 copy-start.1

commit v2 on v1

--- a/solution.py
+++ b/solution.py
@@ -31,9 +31,9 @@
     anc_hbm, panel_hbm, coup_hbm, piv_hbm, lists,
     out_col, out_dia, out_link,
     anc, masked, coup, piv, load_sem,
-    held, via, colbuf, blkbuf, col_a, blk_a, col_b, blk_b, z_in, z_mid,
+    held, colbuf, blkbuf, col_a, blk_a, col_b, blk_b, z_in, z_mid,
     hi_buf, lo_buf,
-    own_up, own_dn, own_rx, via_up, via_dn, via_rx, cross_tx, cross_rx,
+    own_up, own_dn, own_rx,
     cola_tx, cola_rx, blka_tx, blka_rx, colb_tx, colb_rx, blkb_tx, blkb_rx,
     zi_tx, zo_tx, zin_rx, zmid_rx,
 ):
@@ -49,7 +49,6 @@
     x = c // CORES
     k = c % CORES
     mate = x * CORES + (1 - k)
-    other = (x + 1 - 2 * (x % 2)) * CORES + k
     mid = rows // 2
     low = r < mid
     inner = jnp.where(low, r + 1, r - 1)
@@ -103,11 +102,6 @@
                 held[j, s, 0] = masked[s, 0:half, :]
                 held[j, s, 1] = masked[s, half:, :]
 
-        @pl.when(other * q + j == r)
-        def _():
-            for s in range(sups):
-                via[j, s] = masked[s, half:, :]
-
     pl.semaphore_wait(
         barrier,
         jnp.where(r > 0, 1, 0) + jnp.where(r < rows - 1, 1, 0) + nx,
@@ -119,39 +113,38 @@
             device_id={"row": row, "col": col}, device_id_type=MESH,
         )
 
-    def own_copy(j, s, tx, row):
-        ref = held.at[j, s, 0]
-        return remote(ref, ref, tx.at[j, s], own_rx.at[j, s], row, c)
-
-    def via_copy(j, s, tx, row):
-        ref = via.at[j, s]
-        return remote(ref, ref, tx.at[j, s], via_rx.at[j, s], row, c)
-
-    def cross_copy(j, s):
-        return remote(via.at[j, s], held.at[j, s, 1], cross_tx.at[j, s], cross_rx.at[j, s], r, other)
-
-    def service(s):
-        for j in range(q):
-            for maker, first, up, dn, crossing in (
-                (via_copy, other * q + j, via_up, via_dn, True),
-                (own_copy, c * q + j, own_up, own_dn, False),
-            ):
-                @pl.when(first != r)
-                def _():
-                    maker(j, s, up, r).wait_recv()
-
-                @pl.when(jnp.logical_and(first <= r, r < rows - 1))
-                def _():
-                    maker(j, s, up, r + 1).start()
-
-                @pl.when(jnp.logical_and(first >= r, r > 0))
-                def _():
-                    maker(j, s, dn, r - 1).start()
-
-                if crossing:
-                    @pl.when(first != r)
-                    def _():
-                        cross_copy(j, s).start()
+    def own_copy(j, s, h, tx, row):
+        ref = held.at[j, s, h]
+        return remote(ref, ref, tx.at[j, s, h], own_rx.at[j, s, h], row, c)
+
+    chunks = [(j, s, h) for s in range(sups) for j in range(q) for h in range(2)]
+
+    for j, s, h in chunks:
+        @pl.when(jnp.logical_and(c * q + j == r, r < rows - 1))
+        def _():
+            own_copy(j, s, h, own_up, r + 1).start()
+
+        @pl.when(jnp.logical_and(c * q + j == r, r > 0))
+        def _():
+            own_copy(j, s, h, own_dn, r - 1).start()
+
+    def relay(sup):
+        for j, s, h in chunks:
+            if s != sup:
+                continue
+            first = c * q + j
+
+            @pl.when(first != r)
+            def _():
+                own_copy(j, s, h, own_up, r).wait_recv()
+
+            @pl.when(jnp.logical_and(first < r, r < rows - 1))
+            def _():
+                own_copy(j, s, h, own_up, r + 1).start()
+
+            @pl.when(jnp.logical_and(first > r, r > 0))
+            def _():
+                own_copy(j, s, h, own_dn, r - 1).start()
 
     def col_a_copy(s):
         return remote(colbuf.at[s, 1 - k], col_a.at[s], cola_tx.at[s], cola_rx.at[s], r, mate)
@@ -177,10 +170,6 @@
         blk_a_copy(i).start()
 
     def compute(s, before):
-        for j in range(q):
-            @pl.when(c * q + j != r)
-            def _():
-                cross_copy(j, s).wait_recv()
         if s == 0:
             loads[1].wait()
             loads[2].wait()
@@ -231,23 +220,6 @@
         for dx in range(1, nx):
             col_b_copy(s, dx).start()
 
-    service(0)
-    service(1)
-    diag = compute(0, None)
-    service(2)
-    diag = compute(1, diag)
-    blk_to_x(0)
-    for s in range(3, sups):
-        service(s)
-    for s in range(2, sups):
-        diag = compute(s, diag)
-        blk_to_x(2 * s - 3)
-        blk_to_x(2 * s - 2)
-    blk_to_x(pieces - 2)
-    blk_to_x(pieces - 1)
-    for s in range(sups):
-        col_to_x(s)
-
     def to_inner(i, dst, rx):
         return remote(blkbuf.at[i, k, x], dst.at[i], zi_tx.at[i], rx.at[i], inner, c)
 
@@ -292,12 +264,33 @@
         def _():
             to_outer(i).start()
 
-    lag = 2
-    for i in range(pieces + lag):
-        if i < pieces:
+    def names_of(s):
+        return [0] if s == 0 else [2 * s - 1, 2 * s]
+
+    diag = None
+    for s in range(sups):
+        relay(s)
+        diag = compute(s, diag)
+        if s >= 2:
+            for i in names_of(s - 2):
+                z_inward(i)
+        if s >= 1:
+            for i in names_of(s - 1):
+                blk_to_x(i)
+            col_to_x(s - 1)
+        if s >= 3:
+            for i in names_of(s - 3):
+                z_outward(i)
+    for i in names_of(sups - 1):
+        blk_to_x(i)
+    for s in (sups - 2, sups - 1):
+        for i in names_of(s):
             z_inward(i)
-        if i >= lag:
-            z_outward(i - lag)
+        if s == sups - 2:
+            col_to_x(sups - 1)
+    for s in range(max(sups - 3, 0), sups):
+        for i in names_of(s):
+            z_outward(i)
 
     for s in range(sups):
         total = colbuf[s, k, x]
@@ -307,26 +300,18 @@
         out_col[s] = total
 
     for s in range(sups):
-        for j in range(q):
-            for maker, first, up, dn, crossing in (
-                (via_copy, other * q + j, via_up, via_dn, True),
-                (own_copy, c * q + j, own_up, own_dn, False),
-            ):
-                @pl.when(jnp.logical_and(first <= r, r < rows - 1))
-                def _():
-                    maker(j, s, up, r + 1).wait_send()
-
-                @pl.when(jnp.logical_and(first >= r, r > 0))
-                def _():
-                    maker(j, s, dn, r - 1).wait_send()
-
-                if crossing:
-                    @pl.when(first != r)
-                    def _():
-                        cross_copy(j, s).wait_send()
         col_a_copy(s).wait_send()
         for dx in range(1, nx):
             col_b_copy(s, dx).wait_send()
+    for j, s, h in chunks:
+        @pl.when(jnp.logical_and(c * q + j <= r, r < rows - 1))
+        def _():
+            own_copy(j, s, h, own_up, r + 1).wait_send()
+
+        @pl.when(jnp.logical_and(c * q + j >= r, r > 0))
+        def _():
+            own_copy(j, s, h, own_dn, r - 1).wait_send()
+
     for i in range(pieces):
         blk_a_copy(i).wait_send()
         for dx in range(1, nx):
@@ -365,7 +350,6 @@
             pltpu.VMEM(pivots.shape, BF16),
             dma(4),
             pltpu.VMEM((q, sups, 2, half, width), BF16),
-            pltpu.VMEM((q, sups, half, width), BF16),
             pltpu.VMEM((sups, CORES, nx, share, width), F32),
             pltpu.VMEM((pieces, CORES, nx, band, width), F32),
             pltpu.VMEM((sups, nx, share, width), F32),
@@ -376,9 +360,7 @@
             pltpu.VMEM((pieces, band, width), F32),
             pltpu.VMEM((sups, rows_local, width), BF16),
             pltpu.VMEM((sups, rows_local, width), BF16),
-            dma(q, sups), dma(q, sups), dma(q, sups),
-            dma(q, sups), dma(q, sups), dma(q, sups),
-            dma(q, sups), dma(q, sups),
+            dma(q, sups, 2), dma(q, sups, 2), dma(q, sups, 2),
             dma(sups), dma(sups), dma(pieces), dma(pieces),
             dma(sups, nx - 1), dma(sups, nx - 1), dma(pieces, nx - 1), dma(pieces, nx - 1),
             dma(pieces), dma(pieces), dma(pieces), dma(pieces),

time: 128 us -> 71.7 us (0.56)
  Pallas kernels: 123 us -> 67.2 us
    pallas_call x1, Pallas kernels: 123 us -> 67.2 us  [shards(): pl.pallas_call(functools.partial(kernel, rows, cols), out_shape=(jax.Shap...]
where the time goes in v2:
time: 71.7 us; the launch traced here: 71.4 us
  Pallas kernels  67.2 us (94%)
  local copies, waits for them, and re-layouts  3.61 us (5%)
    pallas_call x1, Pallas kernels, shards(): pl.pallas_call(functools.partial(kernel, rows, cols), out_shape=(jax.Shap...  67.2 us
    unnamed x7, local copies, waits for them, and re-layouts  3.61 us

profile of v2, /device:TPU:0, one launch (start us, length us, event | category | flops | bytes accessed | tf_op | source)
XLA Modules:
  0.0 71.4 jit_solution(2058653706608660080)
XLA Ops:
  0.6 67.2 %shard_map.76 = (f32[4,128,256]{2,1,0:T(8,128)}, f32[4,64,256]{2,1,0:T(8,128)}, f32[3,64,256]{2,1,0:T(8,128)}) custom-call(bf16[512,512]{1,0:T(8,128)(2,1)} %anc_hbm.1, bf16[4,512,256]{2,1,0:T(8,128)(2,1)} %panel_hbm.1, bf16[3,256,256]{2,1,0:T(8,128)(2,1)} %coup_hbm.1, bf16[4,256,256]{2,1,0:T(8,128)(2,1)} %piv_hbm.1, s32[4,8]{1,0:T(4,128)} %lists.1), custom_call_target="tpu_custom_call" | custom-call | tf_op jit(solution)/shard_map/pallas_call | solution.py:337
  67.8 0.0 copy-start
  67.8 1.9 %copy.11 = f32[4,128,256]{2,1,0:T(8,128)} copy(f32[4,128,256]{2,1,0:T(8,128)} %get-tuple-element.6) | data formatting | bytes 1048576
  69.7 0.0 copy-done
  69.7 0.0 copy-start.1
  69.7 0.7 copy.12
  70.4 0.3 copy-done.1
  70.8 0.7 copy.13
Async XLA Ops:
  67.8 1.9 %copy-start = (f32[4,64,256]{2,1,0:T(8,128)S(1)}, f32[4,64,256]{2,1,0:T(8,128)}, u32[]{:S(2)}) copy-start(f32[4,64,256]{2,1,0:T(8,128)} %get-tuple-element.7) | copy-start | bytes 786436
  69.7 1.0 %copy-start.1 = (f32[3,64,256]{2,1,0:T(8,128)S(1)}, f32[3,64,256]{2,1,0:T(8,128)}, u32[]{:S(2)}) copy-start(f32[3,64,256]{2,1,0:T(8,128)} %get-tuple-element.8) | copy-start | bytes 589828

commit v3 on v2

--- a/solution.py
+++ b/solution.py
@@ -59,7 +59,8 @@
     loads = [
         pltpu.make_async_copy(src, dst, load_sem.at[i])
         for i, (src, dst) in enumerate(
-            [(panel_hbm, masked), (anc_hbm, anc), (coup_hbm, coup), (piv_hbm, piv)]
+            [(panel_hbm.at[s], masked.at[s]) for s in range(sups)]
+            + [(anc_hbm, anc), (coup_hbm, coup), (piv_hbm, piv)]
         )
     ]
     for load in loads:
@@ -88,20 +89,6 @@
     for t in range(tiles):
         tile = r * tiles + t
         member.append(jnp.max(jnp.where(names == tile, F32(1), F32(0)), axis=1, keepdims=True))
-    loads[0].wait()
-    for s in range(sups):
-        for t in range(tiles):
-            sl = pl.ds(t * width, width)
-            m = member[t][s:s + 1, :].astype(BF16)
-            masked[s, sl, :] = masked[s, sl, :] * m
-
-    for j in range(q):
-        @pl.when(c * q + j == r)
-        def _():
-            for s in range(sups):
-                held[j, s, 0] = masked[s, 0:half, :]
-                held[j, s, 1] = masked[s, half:, :]
-
     pl.semaphore_wait(
         barrier,
         jnp.where(r > 0, 1, 0) + jnp.where(r < rows - 1, 1, 0) + nx,
@@ -119,14 +106,26 @@
 
     chunks = [(j, s, h) for s in range(sups) for j in range(q) for h in range(2)]
 
-    for j, s, h in chunks:
-        @pl.when(jnp.logical_and(c * q + j == r, r < rows - 1))
-        def _():
-            own_copy(j, s, h, own_up, r + 1).start()
-
-        @pl.when(jnp.logical_and(c * q + j == r, r > 0))
-        def _():
-            own_copy(j, s, h, own_dn, r - 1).start()
+    for s in range(sups):
+        loads[s].wait()
+        for t in range(tiles):
+            sl = pl.ds(t * width, width)
+            m = member[t][s:s + 1, :].astype(BF16)
+            masked[s, sl, :] = masked[s, sl, :] * m
+        for j in range(q):
+            @pl.when(c * q + j == r)
+            def _():
+                held[j, s, 0] = masked[s, 0:half, :]
+                held[j, s, 1] = masked[s, half:, :]
+
+                for h in range(2):
+                    @pl.when(r < rows - 1)
+                    def _():
+                        own_copy(j, s, h, own_up, r + 1).start()
+
+                    @pl.when(r > 0)
+                    def _():
+                        own_copy(j, s, h, own_dn, r - 1).start()
 
     def relay(sup):
         for j, s, h in chunks:
@@ -171,9 +170,8 @@
 
     def compute(s, before):
         if s == 0:
-            loads[1].wait()
-            loads[2].wait()
-            loads[3].wait()
+            for load in loads[sups:]:
+                load.wait()
         image = None
         for j in range(q):
             block = held[j, s].reshape(rows_local, width)
@@ -268,36 +266,49 @@
         return [0] if s == 0 else [2 * s - 1, 2 * s]
 
     diag = None
+    relay(0)
     for s in range(sups):
-        relay(s)
         diag = compute(s, diag)
+        if s + 1 < sups:
+            relay(s + 1)
+        for i in names_of(s):
+            blk_to_x(i)
         if s >= 2:
             for i in names_of(s - 2):
                 z_inward(i)
-        if s >= 1:
-            for i in names_of(s - 1):
-                blk_to_x(i)
-            col_to_x(s - 1)
-        if s >= 3:
-            for i in names_of(s - 3):
-                z_outward(i)
-    for i in names_of(sups - 1):
-        blk_to_x(i)
-    for s in (sups - 2, sups - 1):
-        for i in names_of(s):
-            z_inward(i)
-        if s == sups - 2:
-            col_to_x(sups - 1)
-    for s in range(max(sups - 3, 0), sups):
-        for i in names_of(s):
-            z_outward(i)
-
-    for s in range(sups):
+        if s < sups - 1:
+            col_to_x(s)
+
+    def finish(s):
         total = colbuf[s, k, x]
         for dx in range(1, nx):
             col_b_copy(s, dx).wait_recv()
             total = total + col_b[s, dx - 1]
         out_col[s] = total
+
+    col_to_x(sups - 1)
+    begun = pieces - 4
+
+    @pl.when(has_outer)
+    def _():
+        behind = 0
+        for i in range(begun, pieces):
+            z_inward(i)
+            while behind < i - 1:
+                z_outward(behind)
+                behind += 1
+        for i in range(behind, pieces):
+            z_outward(i)
+
+    @pl.when(jnp.logical_not(has_outer))
+    def _():
+        for i in range(begun, pieces):
+            z_inward(i)
+        for i in range(pieces):
+            z_outward(i)
+
+    for s in range(sups):
+        finish(s)
 
     for s in range(sups):
         col_a_copy(s).wait_send()
@@ -348,7 +359,7 @@
             pltpu.VMEM(panel.shape, BF16),
             pltpu.VMEM(coupling.shape, BF16),
             pltpu.VMEM(pivots.shape, BF16),
-            dma(4),
+            dma(sups + 3),
             pltpu.VMEM((q, sups, 2, half, width), BF16),
             pltpu.VMEM((sups, CORES, nx, share, width), F32),
             pltpu.VMEM((pieces, CORES, nx, band, width), F32),

time: 71.7 us -> 61.5 us (0.86)
  Pallas kernels: 67.2 us -> 57.1 us
    pallas_call x1, Pallas kernels: 67.2 us -> 57.1 us  [shards(): pl.pallas_call(functools.partial(kernel, rows, cols), out_shape=(jax.Shap...]
where the time goes in v3:
time: 61.5 us; the launch traced here: 61.3 us
  Pallas kernels  57.1 us (93%)
  local copies, waits for them, and re-layouts  3.61 us (6%)
  between operations  0.65 us (1%)
    pallas_call x1, Pallas kernels, shards(): pl.pallas_call(functools.partial(kernel, rows, cols), out_shape=(jax.Shap...  57.1 us
    unnamed x7, local copies, waits for them, and re-layouts  3.61 us

profile of v3, /device:TPU:0, one launch (start us, length us, event | category | flops | bytes accessed | tf_op | source)
XLA Modules:
  0.0 61.3 jit_solution(14895534734847240810)
XLA Ops:
  0.6 57.1 %shard_map.76 = (f32[4,128,256]{2,1,0:T(8,128)}, f32[4,64,256]{2,1,0:T(8,128)}, f32[3,64,256]{2,1,0:T(8,128)}) custom-call(bf16[512,512]{1,0:T(8,128)(2,1)} %anc_hbm.1, bf16[4,512,256]{2,1,0:T(8,128)(2,1)} %panel_hbm.1, bf16[3,256,256]{2,1,0:T(8,128)(2,1)} %coup_hbm.1, bf16[4,256,256]{2,1,0:T(8,128)(2,1)} %piv_hbm.1, s32[4,8]{1,0:T(4,128)} %lists.1), custom_call_target="tpu_custom_call" | custom-call | tf_op jit(solution)/shard_map/pallas_call | solution.py:348
  57.7 0.0 copy-start
  57.7 1.9 %copy.11 = f32[4,128,256]{2,1,0:T(8,128)} copy(f32[4,128,256]{2,1,0:T(8,128)} %get-tuple-element.6) | data formatting | bytes 1048576
  59.6 0.0 copy-done
  59.6 0.0 copy-start.1
  59.6 0.7 %copy.12 = f32[4,64,256]{2,1,0:T(8,128)} copy(f32[4,64,256]{2,1,0:T(8,128)S(1)} %copy-done) | data formatting | bytes 524288
  60.3 0.3 copy-done.1
  60.6 0.7 %copy.13 = f32[3,64,256]{2,1,0:T(8,128)} copy(f32[3,64,256]{2,1,0:T(8,128)S(1)} %copy-done.1) | data formatting | bytes 393216
Async XLA Ops:
  57.7 1.9 %copy-start = (f32[4,64,256]{2,1,0:T(8,128)S(1)}, f32[4,64,256]{2,1,0:T(8,128)}, u32[]{:S(2)}) copy-start(f32[4,64,256]{2,1,0:T(8,128)} %get-tuple-element.7) | copy-start | bytes 786436
  59.6 1.0 %copy-start.1 = (f32[3,64,256]{2,1,0:T(8,128)S(1)}, f32[3,64,256]{2,1,0:T(8,128)}, u32[]{:S(2)}) copy-start(f32[3,64,256]{2,1,0:T(8,128)} %get-tuple-element.8) | copy-start | bytes 589828

commit v4 on v3

--- a/solution.py
+++ b/solution.py
@@ -11,6 +11,7 @@
 BF16 = jnp.bfloat16
 MESH = pl.DeviceIdType.MESH
 CORES = 2
+PARTS = 4
 
 
 def dot(a, b):
@@ -38,7 +39,7 @@
     zi_tx, zo_tx, zin_rx, zmid_rx,
 ):
     sups, rows_local, width = masked.shape
-    half = rows_local // 2
+    half = rows_local // PARTS
     q = rows // cols
     nx = cols // CORES
     share = rows_local // cols
@@ -104,7 +105,7 @@
         ref = held.at[j, s, h]
         return remote(ref, ref, tx.at[j, s, h], own_rx.at[j, s, h], row, c)
 
-    chunks = [(j, s, h) for s in range(sups) for j in range(q) for h in range(2)]
+    chunks = [(j, s, h) for s in range(sups) for j in range(q) for h in range(PARTS)]
 
     for s in range(sups):
         loads[s].wait()
@@ -115,10 +116,10 @@
         for j in range(q):
             @pl.when(c * q + j == r)
             def _():
-                held[j, s, 0] = masked[s, 0:half, :]
-                held[j, s, 1] = masked[s, half:, :]
-
-                for h in range(2):
+                for h in range(PARTS):
+                    held[j, s, h] = masked[s, h * half:(h + 1) * half, :]
+
+                for h in range(PARTS):
                     @pl.when(r < rows - 1)
                     def _():
                         own_copy(j, s, h, own_up, r + 1).start()
@@ -341,7 +342,7 @@
     share = rows_local // cols
     band = width // cols
     pieces = 2 * sups - 1
-    half = rows_local // 2
+    half = rows_local // PARTS
     dma = lambda *shape: pltpu.SemaphoreType.DMA(shape)
     hbm = pl.BlockSpec(memory_space=pl.ANY)
     vmem = pl.BlockSpec(memory_space=pltpu.VMEM)
@@ -360,7 +361,7 @@
             pltpu.VMEM(coupling.shape, BF16),
             pltpu.VMEM(pivots.shape, BF16),
             dma(sups + 3),
-            pltpu.VMEM((q, sups, 2, half, width), BF16),
+            pltpu.VMEM((q, sups, PARTS, half, width), BF16),
             pltpu.VMEM((sups, CORES, nx, share, width), F32),
             pltpu.VMEM((pieces, CORES, nx, band, width), F32),
             pltpu.VMEM((sups, nx, share, width), F32),
@@ -371,7 +372,7 @@
             pltpu.VMEM((pieces, band, width), F32),
             pltpu.VMEM((sups, rows_local, width), BF16),
             pltpu.VMEM((sups, rows_local, width), BF16),
-            dma(q, sups, 2), dma(q, sups, 2), dma(q, sups, 2),
+            dma(q, sups, PARTS), dma(q, sups, PARTS), dma(q, sups, PARTS),
             dma(sups), dma(sups), dma(pieces), dma(pieces),
             dma(sups, nx - 1), dma(sups, nx - 1), dma(pieces, nx - 1), dma(pieces, nx - 1),
             dma(pieces), dma(pieces), dma(pieces), dma(pieces),

time: 61.5 us -> 60.7 us (0.987)
  Pallas kernels: 57.1 us -> 56.2 us
    pallas_call x1, Pallas kernels: 57.1 us -> 56.2 us  [shards(): pl.pallas_call(functools.partial(kernel, rows, cols), out_shape=(jax.Shap...]
where the time goes in v4:
time: 60.7 us; the launch traced here: 60.5 us
  Pallas kernels  56.2 us (93%)
  local copies, waits for them, and re-layouts  3.61 us (6%)
  between operations  0.65 us (1%)
    pallas_call x1, Pallas kernels, shards(): pl.pallas_call(functools.partial(kernel, rows, cols), out_shape=(jax.Shap...  56.2 us
    unnamed x7, local copies, waits for them, and re-layouts  3.61 us

profile of v4, /device:TPU:0, one launch (start us, length us, event | category | flops | bytes accessed | tf_op | source)
XLA Modules:
  0.0 60.5 jit_solution(6478224011584504308)
XLA Ops:
  0.6 56.2 %shard_map.76 = (f32[4,128,256]{2,1,0:T(8,128)}, f32[4,64,256]{2,1,0:T(8,128)}, f32[3,64,256]{2,1,0:T(8,128)}) custom-call(bf16[512,512]{1,0:T(8,128)(2,1)} %anc_hbm.1, bf16[4,512,256]{2,1,0:T(8,128)(2,1)} %panel_hbm.1, bf16[3,256,256]{2,1,0:T(8,128)(2,1)} %coup_hbm.1, bf16[4,256,256]{2,1,0:T(8,128)(2,1)} %piv_hbm.1, s32[4,8]{1,0:T(4,128)} %lists.1), custom_call_target="tpu_custom_call" | custom-call | tf_op jit(solution)/shard_map/pallas_call | solution.py:349
  56.9 0.0 copy-start
  56.9 1.9 %copy.11 = f32[4,128,256]{2,1,0:T(8,128)} copy(f32[4,128,256]{2,1,0:T(8,128)} %get-tuple-element.6) | data formatting | bytes 1048576
  58.8 0.0 copy-done
  58.8 0.0 copy-start.1
  58.8 0.7 %copy.12 = f32[4,64,256]{2,1,0:T(8,128)} copy(f32[4,64,256]{2,1,0:T(8,128)S(1)} %copy-done) | data formatting | bytes 524288
  59.5 0.3 copy-done.1
  59.8 0.7 %copy.13 = f32[3,64,256]{2,1,0:T(8,128)} copy(f32[3,64,256]{2,1,0:T(8,128)S(1)} %copy-done.1) | data formatting | bytes 393216
Async XLA Ops:
  56.9 1.9 %copy-start = (f32[4,64,256]{2,1,0:T(8,128)S(1)}, f32[4,64,256]{2,1,0:T(8,128)}, u32[]{:S(2)}) copy-start(f32[4,64,256]{2,1,0:T(8,128)} %get-tuple-element.7) | copy-start | bytes 786436
  58.8 1.0 %copy-start.1 = (f32[3,64,256]{2,1,0:T(8,128)S(1)}, f32[3,64,256]{2,1,0:T(8,128)}, u32[]{:S(2)}) copy-start(f32[3,64,256]{2,1,0:T(8,128)} %get-tuple-element.8) | copy-start | bytes 589828
